TPU v7x, 128 devices: a whole 4x4x4 slice. The times are simulated.
128 devices in a mesh: dp: 8 (over z_hi, y), tensor: 16 (over x, z_lo, core).
Axes of the slice: x: 4, y: 4, z: 4 (z_hi: 2, z_lo: 2; z = z_hi * 2 + z_lo), core: 2. Of those that a mesh axis runs over, the one named last changes fastest.
Arguments:
- tokens: bfloat16 [16, 1024, 2048], P('dp', 'tensor'), may hold values from -6 to 6
- attn_weight: bfloat16 [2048, 6144], P('dp', 'tensor'), may hold values from -0.125 to 0.125
- attn_bias: float32 [6144], P('tensor'), may hold values from -3 to 3
- dense_weight: bfloat16 [2048, 2048], P('tensor', 'dp'), may hold values from -0.75 to 0.75
- dense_bias: float32 [2048], replicated, may hold values from -3 to 3
- up_weight: bfloat16 [2048, 8192], P('dp', 'tensor'), may hold values from -0.125 to 0.125
- up_bias: float32 [8192], P('tensor'), may hold values from -3 to 3
- down_weight: bfloat16 [8192, 2048], P('tensor', 'dp'), may hold values from -0.0625 to 0.0625
- down_bias: float32 [2048], replicated, may hold values from -3 to 3
- norm_gain: float32 [2048], replicated, may hold values from 0.5 to 1.5
- norm_bias: float32 [2048], replicated, may hold values from -2 to 2
- cotangent: bfloat16 [16, 1024, 2048], P('dp', 'tensor'), may hold values from -6 to 6
Outputs:
- layer_out: bfloat16 [16, 1024, 2048], P('dp', 'tensor')
- grad_tokens: float32 [16, 1024, 2048], P('dp', 'tensor')
- attn_weight_grad: float32 [2048, 6144], P('dp', 'tensor')
- attn_bias_grad: float32 [6144], P('tensor')
- dense_weight_grad: float32 [2048, 2048], P('tensor', 'dp')
- dense_bias_grad: float32 [2048], replicated
- up_weight_grad: float32 [2048, 8192], P('dp', 'tensor')
- up_bias_grad: float32 [8192], P('tensor')
- down_weight_grad: float32 [8192, 2048], P('tensor', 'dp')
- down_bias_grad: float32 [2048], replicated
- norm_gain_grad: float32 [2048], replicated
- norm_bias_grad: float32 [2048], replicated
All inputs are finite; a program needn't handle non-finite values.
Results may differ from a plain program's by a relative error of at most 0.0089.
Values may be sent and summed in bfloat16 or wider, within the bound.
No kernel may reach another device: no remote copies, remote signals or barrier semaphores. Data moves between devices by JAX's collectives and lax.ppermute only.
A program may use at most 192 MiB of HBM per device.

v0:
```python
import jax
import jax.numpy as jnp
from jax import lax
from jax.sharding import PartitionSpec as P

HEAD_DIM = 64
ROT = 32
BLOCK = 512


epsilon = 1e-05


def normalize(rows_in, norm_gain, norm_bias):
    average = jnp.mean(rows_in, axis=-1, keepdims=True)
    centred = rows_in - average
    spread = jnp.mean(centred * centred, axis=-1, keepdims=True)
    return centred * lax.rsqrt(spread + epsilon) * norm_gain + norm_bias


def activate(pre_active):
    return jax.nn.gelu(pre_active, approximate=True)


def rotary_tables(length):
    half_rot = ROT // 2
    frequency = 10000.0 ** (-(jnp.arange(half_rot, dtype=jnp.float32) * 2.0 / ROT))
    angles = jnp.arange(length, dtype=jnp.float32)[:, None] * frequency[None, :]
    return (jnp.cos(angles), jnp.sin(angles))


def rotate(operand, cosine_table, sine_table, direction):
    half_rot = ROT // 2
    first_half = operand[..., :half_rot]
    second_half = operand[..., half_rot:ROT]
    return jnp.concatenate(
        [
            first_half * cosine_table - direction * (second_half * sine_table),
            second_half * cosine_table + direction * (first_half * sine_table),
            operand[..., ROT:],
        ],
        axis=-1,
    )


def contract_rows(left, right):
    return lax.dot_general(
        left, right, (((0,), (0,)), ((), ())), preferred_element_type=jnp.float32
    )


def contract_cols(left, right):
    return lax.dot_general(
        left, right, (((1,), (1,)), ((), ())), preferred_element_type=jnp.float32
    )


def causal_scores(query_rows, keys_all, row_begin, factor):
    row_count = query_rows.shape[1]
    row_finish = row_begin + row_count
    scores = (
        jnp.einsum(
            "hqd,hkd->hqk", query_rows, keys_all[:, :row_finish], preferred_element_type=jnp.float32
        )
        * factor
    )
    allowed = jnp.arange(row_finish)[None, :] <= (row_begin + jnp.arange(row_count))[:, None]
    return jnp.where(allowed, scores, -jnp.inf)


def shards(
    tokens,
    attn_weight,
    attn_bias,
    dense_weight,
    dense_bias,
    up_weight,
    up_bias,
    down_weight,
    down_bias,
    norm_gain,
    norm_bias,
    cotangent,
):
    local_rows = tokens.shape[1]
    model_width = tokens.shape[2]
    length = local_rows * lax.axis_size("tensor")
    heads_here = attn_weight.shape[1] // (3 * HEAD_DIM)
    factor = HEAD_DIM ** (-0.5)
    cosine_table, sine_table = rotary_tables(length)
    blocks = length // BLOCK

    def micro_step(state_in, inputs):
        (
            acc_attn,
            acc_up,
            acc_dense,
            acc_down,
            acc_attn_bias,
            acc_up_bias,
            acc_gain,
            acc_norm_bias,
            acc_out_bias,
        ) = state_in
        seq_rows, seq_cot = inputs
        rows_in = seq_rows.astype(jnp.float32)
        normed, norm_back = jax.vjp(normalize, rows_in, norm_gain, norm_bias)
        activations = lax.all_gather(normed.astype(jnp.bfloat16), "tensor", axis=0, tiled=True)
        forward_weights = (
            lax.all_gather(attn_weight, "dp", axis=0, tiled=True),
            lax.all_gather(up_weight, "dp", axis=0, tiled=True),
            lax.all_gather(dense_weight, "dp", axis=1, tiled=True),
            lax.all_gather(down_weight, "dp", axis=1, tiled=True),
        )
        full_attn, full_up, full_dense, full_down = forward_weights
        projected = jnp.dot(activations, full_attn, preferred_element_type=jnp.float32) + attn_bias
        shaped = projected.reshape(length, heads_here, 3, HEAD_DIM).transpose(2, 1, 0, 3)
        queries = rotate(shaped[0], cosine_table, sine_table, 1.0).astype(jnp.bfloat16)
        keys_all = rotate(shaped[1], cosine_table, sine_table, 1.0).astype(jnp.bfloat16)
        values_all = shaped[2].astype(jnp.bfloat16)
        pieces = []
        log_totals = []
        for block_index in range(blocks):
            row_begin = block_index * BLOCK
            row_finish = row_begin + BLOCK
            scores = causal_scores(queries[:, row_begin:row_finish], keys_all, row_begin, factor)
            row_max = jnp.max(scores, axis=-1, keepdims=True)
            exponent = jnp.exp(scores - row_max)
            row_total = jnp.sum(exponent, axis=-1, keepdims=True)
            probab = (exponent / row_total).astype(jnp.bfloat16)
            pieces.append(
                jnp.einsum(
                    "hqk,hkd->hqd",
                    probab,
                    values_all[:, :row_finish],
                    preferred_element_type=jnp.float32,
                )
            )
            log_totals.append(row_max + jnp.log(row_total))
        attended = jnp.concatenate(pieces, axis=1)
        merged = (
            attended.transpose(1, 0, 2).reshape(length, heads_here * HEAD_DIM).astype(jnp.bfloat16)
        )
        attn_part = jnp.dot(merged, full_dense, preferred_element_type=jnp.float32)
        hidden = jnp.dot(activations, full_up, preferred_element_type=jnp.float32) + up_bias
        active_full, gelu_back = jax.vjp(activate, hidden)
        active = active_full.astype(jnp.bfloat16)
        partial_out = attn_part + jnp.dot(active, full_down, preferred_element_type=jnp.float32)
        branch = lax.psum_scatter(partial_out, "tensor", scatter_dimension=0, tiled=True)
        layer_rows = (rows_in + branch + dense_bias + down_bias).astype(jnp.bfloat16)
        grad_out = lax.all_gather(seq_cot, "tensor", axis=0, tiled=True)
        backward_weights = (
            lax.all_gather(attn_weight, "dp", axis=0, tiled=True),
            lax.all_gather(up_weight, "dp", axis=0, tiled=True),
            lax.all_gather(dense_weight, "dp", axis=1, tiled=True),
            lax.all_gather(down_weight, "dp", axis=1, tiled=True),
        )
        back_attn, back_up, back_dense, back_down = backward_weights
        acc_dense = acc_dense + contract_rows(merged, grad_out)
        acc_down = acc_down + contract_rows(active, grad_out)
        grad_merged = contract_cols(grad_out, back_dense).astype(jnp.bfloat16)
        grad_hidden = gelu_back(contract_cols(grad_out, back_down))[0].astype(jnp.bfloat16)
        acc_up_bias = acc_up_bias + jnp.sum(grad_hidden.astype(jnp.float32), axis=0)
        acc_up = acc_up + contract_rows(activations, grad_hidden)
        unit_grad_acts = contract_cols(grad_hidden, back_up)
        grad_heads = grad_merged.reshape(length, heads_here, HEAD_DIM).transpose(1, 0, 2)
        query_grads = []
        key_grad = jnp.zeros((heads_here, length, HEAD_DIM), jnp.float32)
        value_grad = jnp.zeros((heads_here, length, HEAD_DIM), jnp.float32)
        for block_index in range(blocks):
            row_begin = block_index * BLOCK
            row_finish = row_begin + BLOCK
            query_rows = queries[:, row_begin:row_finish]
            grad_rows = grad_heads[:, row_begin:row_finish]
            scores = causal_scores(query_rows, keys_all, row_begin, factor)
            probab = jnp.exp(scores - log_totals[block_index])
            grad_probab = jnp.einsum(
                "hqd,hkd->hqk",
                grad_rows,
                values_all[:, :row_finish],
                preferred_element_type=jnp.float32,
            )
            row_delta = jnp.sum(probab * grad_probab, axis=-1, keepdims=True)
            grad_scores = (probab * (grad_probab - row_delta)).astype(jnp.bfloat16)
            query_grads.append(
                jnp.einsum(
                    "hqk,hkd->hqd",
                    grad_scores,
                    keys_all[:, :row_finish],
                    preferred_element_type=jnp.float32,
                )
                * factor
            )
            key_grad = key_grad.at[:, :row_finish].add(
                jnp.einsum(
                    "hqk,hqd->hkd", grad_scores, query_rows, preferred_element_type=jnp.float32
                )
                * factor
            )
            value_grad = value_grad.at[:, :row_finish].add(
                jnp.einsum(
                    "hqk,hqd->hkd",
                    probab.astype(jnp.bfloat16),
                    grad_rows,
                    preferred_element_type=jnp.float32,
                )
            )
        query_grad = rotate(jnp.concatenate(query_grads, axis=1), cosine_table, sine_table, -1.0)
        key_grad = rotate(key_grad, cosine_table, sine_table, -1.0)
        grad_projected = jnp.stack([query_grad, key_grad, value_grad], axis=0).transpose(2, 1, 0, 3)
        grad_projected = grad_projected.reshape(length, 3 * heads_here * HEAD_DIM).astype(
            jnp.bfloat16
        )
        acc_attn_bias = acc_attn_bias + jnp.sum(grad_projected.astype(jnp.float32), axis=0)
        acc_attn = acc_attn + contract_rows(activations, grad_projected)
        head_grad_acts = contract_cols(grad_projected, back_attn)
        grad_normed = lax.psum_scatter(
            unit_grad_acts + head_grad_acts, "tensor", scatter_dimension=0, tiled=True
        )
        grad_rows_in, grad_gain, grad_norm_bias = norm_back(grad_normed)
        cot_rows = seq_cot.astype(jnp.float32)
        state_out = (
            acc_attn,
            acc_up,
            acc_dense,
            acc_down,
            acc_attn_bias,
            acc_up_bias,
            acc_gain + grad_gain,
            acc_norm_bias + grad_norm_bias,
            acc_out_bias + jnp.sum(cot_rows, axis=0),
        )
        return (state_out, (layer_rows, cot_rows + grad_rows_in))

    initial = (
        jnp.zeros((model_width, attn_weight.shape[1]), jnp.float32),
        jnp.zeros((model_width, up_weight.shape[1]), jnp.float32),
        jnp.zeros((dense_weight.shape[0], model_width), jnp.float32),
        jnp.zeros((down_weight.shape[0], model_width), jnp.float32),
        jnp.zeros((attn_weight.shape[1],), jnp.float32),
        jnp.zeros((up_weight.shape[1],), jnp.float32),
        jnp.zeros((model_width,), jnp.float32),
        jnp.zeros((model_width,), jnp.float32),
        jnp.zeros((model_width,), jnp.float32),
    )
    final_state, stacked = lax.scan(micro_step, initial, (tokens, cotangent))
    (
        acc_attn,
        acc_up,
        acc_dense,
        acc_down,
        acc_attn_bias,
        acc_up_bias,
        acc_gain,
        acc_norm_bias,
        acc_out_bias,
    ) = final_state
    layer_out, grad_tokens = stacked
    attn_grad, up_grad, dense_grad, down_grad = (
        lax.psum_scatter(acc_attn, "dp", scatter_dimension=0, tiled=True),
        lax.psum_scatter(acc_up, "dp", scatter_dimension=0, tiled=True),
        lax.psum_scatter(acc_dense, "dp", scatter_dimension=1, tiled=True),
        lax.psum_scatter(acc_down, "dp", scatter_dimension=1, tiled=True),
    )
    attn_bias_grad, up_bias_grad = lax.psum((acc_attn_bias, acc_up_bias), "dp")
    gain_grad, norm_bias_grad, out_bias_grad = lax.psum(
        (acc_gain, acc_norm_bias, acc_out_bias), ("dp", "tensor")
    )
    return (
        layer_out,
        grad_tokens,
        attn_grad,
        attn_bias_grad,
        dense_grad,
        out_bias_grad,
        up_grad,
        up_bias_grad,
        down_grad,
        out_bias_grad,
        gain_grad,
        norm_bias_grad,
    )


def solution(mesh):
    in_specs = (
        P("dp", "tensor", None),
        P("dp", "tensor"),
        P("tensor"),
        P("tensor", "dp"),
        P(),
        P("dp", "tensor"),
        P("tensor"),
        P("tensor", "dp"),
        P(),
        P(),
        P(),
        P("dp", "tensor", None),
    )
    out_specs = (
        P("dp", "tensor", None),
        P("dp", "tensor", None),
        P("dp", "tensor"),
        P("tensor"),
        P("tensor", "dp"),
        P(),
        P("dp", "tensor"),
        P("tensor"),
        P("tensor", "dp"),
        P(),
        P(),
        P(),
    )
    return jax.shard_map(shards, mesh=mesh, in_specs=in_specs, out_specs=out_specs, check_vma=False)
```

profile of v0, /device:TPU:24, one launch (start us, length us, event | category | flops | bytes accessed | tf_op | source)
XLA Modules:
  0.0 1284.6 jit_solution(3938492188294096148)
XLA Ops:
  8.1 928.5 %while.43 = (s32[]{:T(128)}, f32[2048,384]{1,0:T(8,128)}, f32[2048,512]{1,0:T(8,128)}, f32[128,2048]{1,0:T(8,128)}, f32[512,2048]{1,0:T(8,128)}, /*index=5*/f32[...) while((s32[]{:T(128)}, f32[2048,384]{1,0:T(8,128)}, ...), condition=%wide.region_18.19_spmd.clone.clone.clone.clone, body=%wide.region_0.18_spmd.clone.clone.clone.clone.sunk | while | flops 20612796416 | bytes 560719296 | solution.py:246
  19.2 35.4 %all_gather.74 = bf16[128,2048]{1,0:T(8,128)(2,1)S(1)} all-gather(bf16[128,256]{1,0:T(8,128)(2,1)S(1)} %copy-done.30), channel_id=1, replica_groups=mesh['dp'=8,'tensor'=16] {'dp'}, dimensions={1}, use_global_device_ids=true | all-gather | bytes 589824 | tf_op jit(solution)/shard_map/while/body/eval_jaxpr/all_gather | solution.py:155
  54.7 11.9 all-gather.14.cloned.1.call-done
  66.6 38.9 %all-gather.12.cloned.1.call-done = bf16[1024,2048]{1,0:T(8,128)(2,1)} async-done(((bf16[64,2048]{1,0:T(8,128)(2,1)}), bf16[1024,2048]{1,0:T(8,128)(2,1)}) %all-gather.12.cloned.1.call-update) | async-done | bytes 4194320 | tf_op jit(solution)/shard_map/while/body/eval_jaxpr/all_gather | solution.py:108
  116.2 28.5 %all-gather.16.cloned.1.call-done = bf16[1,1024,2048]{2,1,0:T(8,128)(2,1)} async-done(((bf16[1,64,2048]{2,1,0:T(8,128)(2,1)}), bf16[1,1024,2048]{2,1,0:T(8,128)(2,1)}) %all-gather.16.cloned.1.call-update) | async-done | bytes 4194320 | tf_op jit(solution)/shard_map/while/body/eval_jaxpr/all_gather | solution.py:151
  156.9 44.8 %all-gather.18.cloned.1.call-done = bf16[2048,512]{1,0:T(8,128)(2,1)} async-done(((bf16[256,512]{1,0:T(8,128)(2,1)}), bf16[2048,512]{1,0:T(8,128)(2,1)}) %all-gather.18.cloned.1.call-update) | async-done | bytes 2097168 | tf_op jit(solution)/shard_map/while/body/eval_jaxpr/all_gather | solution.py:111
  208.8 51.3 %all-gather.20.cloned.1.call-done = bf16[512,2048]{1,0:T(8,128)(2,1)} async-done(((bf16[512,256]{1,0:T(8,128)(2,1)}), bf16[512,2048]{1,0:T(8,128)(2,1)}) %all-gather.20.cloned.1.call-update) | async-done | bytes 2097168 | tf_op jit(solution)/shard_map/while/body/eval_jaxpr/all_gather | solution.py:156
  260.0 7.2 convert_reduce_fusion.10
  310.6 58.4 %reduce-scatter.15.cloned.1.call-done = f32[64,2048]{1,0:T(8,128)} async-done(((f32[1024,2048]{1,0:T(8,128)}), f32[64,2048]{1,0:T(8,128)}) %reduce-scatter.15.cloned.1.call-update) | async-done | bytes 524304 | tf_op jit(solution)/shard_map/while/body/eval_jaxpr/reduce_scatter | solution.py:217
  373.3 95.7 %reduce-scatter.17.cloned.1.call-done = f32[64,2048]{1,0:T(8,128)} async-done(((f32[1024,2048]{1,0:T(8,128)}), f32[64,2048]{1,0:T(8,128)}) %reduce-scatter.17.cloned.1.call-update) | async-done | bytes 524304 | tf_op jit(solution)/shard_map/while/body/eval_jaxpr/reduce_scatter | solution.py:149
  482.3 35.6 %all_gather.74 = bf16[128,2048]{1,0:T(8,128)(2,1)S(1)} all-gather(bf16[128,256]{1,0:T(8,128)(2,1)S(1)} %copy-done.30), channel_id=1, replica_groups=mesh['dp'=8,'tensor'=16] {'dp'}, dimensions={1}, use_global_device_ids=true | all-gather | bytes 589824 | tf_op jit(solution)/shard_map/while/body/eval_jaxpr/all_gather | solution.py:155
  517.9 12.4 all-gather.14.cloned.1.call-done
  530.3 39.0 %all-gather.12.cloned.1.call-done = bf16[1024,2048]{1,0:T(8,128)(2,1)} async-done(((bf16[64,2048]{1,0:T(8,128)(2,1)}), bf16[1024,2048]{1,0:T(8,128)(2,1)}) %all-gather.12.cloned.1.call-update) | async-done | bytes 4194320 | tf_op jit(solution)/shard_map/while/body/eval_jaxpr/all_gather | solution.py:108
  579.9 28.3 %all-gather.16.cloned.1.call-done = bf16[1,1024,2048]{2,1,0:T(8,128)(2,1)} async-done(((bf16[1,64,2048]{2,1,0:T(8,128)(2,1)}), bf16[1,1024,2048]{2,1,0:T(8,128)(2,1)}) %all-gather.16.cloned.1.call-update) | async-done | bytes 4194320 | tf_op jit(solution)/shard_map/while/body/eval_jaxpr/all_gather | solution.py:151
  620.4 45.0 %all-gather.18.cloned.1.call-done = bf16[2048,512]{1,0:T(8,128)(2,1)} async-done(((bf16[256,512]{1,0:T(8,128)(2,1)}), bf16[2048,512]{1,0:T(8,128)(2,1)}) %all-gather.18.cloned.1.call-update) | async-done | bytes 2097168 | tf_op jit(solution)/shard_map/while/body/eval_jaxpr/all_gather | solution.py:111
  672.2 51.6 %all-gather.20.cloned.1.call-done = bf16[512,2048]{1,0:T(8,128)(2,1)} async-done(((bf16[512,256]{1,0:T(8,128)(2,1)}), bf16[512,2048]{1,0:T(8,128)(2,1)}) %all-gather.20.cloned.1.call-update) | async-done | bytes 2097168 | tf_op jit(solution)/shard_map/while/body/eval_jaxpr/all_gather | solution.py:156
  769.6 7.3 select_add_fusion.17
  776.9 55.8 %reduce-scatter.15.cloned.1.call-done = f32[64,2048]{1,0:T(8,128)} async-done(((f32[1024,2048]{1,0:T(8,128)}), f32[64,2048]{1,0:T(8,128)}) %reduce-scatter.15.cloned.1.call-update) | async-done | bytes 524304 | tf_op jit(solution)/shard_map/while/body/eval_jaxpr/reduce_scatter | solution.py:217
  837.1 95.5 %reduce-scatter.17.cloned.1.call-done = f32[64,2048]{1,0:T(8,128)} async-done(((f32[1024,2048]{1,0:T(8,128)}), f32[64,2048]{1,0:T(8,128)}) %reduce-scatter.17.cloned.1.call-update) | async-done | bytes 524304 | tf_op jit(solution)/shard_map/while/body/eval_jaxpr/reduce_scatter | solution.py:149
  939.2 69.0 %all-reduce.2 = (f32[2048]{0:T(1024)S(1)}, f32[2048]{0:T(1024)}, f32[2048]{0:T(1024)}) all-reduce(f32[2048]{0:T(1024)S(1)} %copy-done.44, f32[2048]{0:T(1024)S(1)} %copy-done.50, f32[2048]{0:T(1024)S(1)} %copy-done.47), channel_id=1, replica_groups=mesh['dp'=8,'tensor'=16] {'dp','tensor'}, use_global_device_ids=true, to_apply=%region_22.23 | all-reduce | flops 6144 | bytes 49152 | tf_op jit(solution)/shard_map/psum | solution.py:266
  1008.2 19.3 %all-reduce.3 = (f32[384]{0:T(512)}, f32[512]{0:T(512)}) all-reduce(f32[384]{0:T(512)S(1)} %copy-done.60, f32[512]{0:T(512)S(1)} %copy-done.57), channel_id=1, replica_groups=mesh['dp'=8,'tensor'=16] {'dp'}, use_global_device_ids=true, to_apply=%region_20.21 | all-reduce | flops 896 | bytes 7168 | tf_op jit(solution)/shard_map/psum | solution.py:265
  1027.5 72.9 %reduce-scatter.7.cloned.1.call-done = f32[256,384]{1,0:T(8,128)} async-done(((f32[2048,384]{1,0:T(8,128)}), f32[256,384]{1,0:T(8,128)}) %reduce-scatter.7.cloned.1.call-update) | async-done | bytes 393232 | tf_op jit(solution)/shard_map/reduce_scatter | solution.py:260
  1100.4 87.8 %reduce-scatter.11.cloned.1.call-done = f32[256,512]{1,0:T(8,128)} async-done(((f32[2048,512]{1,0:T(8,128)}), f32[256,512]{1,0:T(8,128)}) %reduce-scatter.11.cloned.1.call-update) | async-done | bytes 524304 | tf_op jit(solution)/shard_map/reduce_scatter | solution.py:261
  1188.2 88.1 %reduce-scatter.13.cloned.1.call-done = f32[512,256]{1,0:T(8,128)} async-done(((f32[512,2048]{1,0:T(8,128)}), f32[512,256]{1,0:T(8,128)}) %reduce-scatter.13.cloned.1.call-update) | async-done | bytes 524304 | tf_op jit(solution)/shard_map/reduce_scatter | solution.py:263
  (476 shorter events, 184.1 us)
Async XLA Ops:
  8.4 58.2 %all-gather.14.cloned.1.call-start = ((), (), s32[]{:S(2)}) async-start(), calls=%async_computation.11 | async-start | bytes 1769472 | tf_op jit(solution)/shard_map/while/body/eval_jaxpr/all_gather | solution.py:110
  9.2 96.3 %all-gather.12.cloned.1.call-start = ((), (), s32[]{:S(2)}) async-start(), calls=%async_computation.10 | async-start | bytes 4456448 | tf_op jit(solution)/shard_map/while/body/eval_jaxpr/all_gather | solution.py:108
  14.0 130.7 %all-gather.16.cloned.1.call-start = ((), (), s32[]{:S(2)}) async-start(), calls=%async_computation.12 | async-start | bytes 4456448 | tf_op jit(solution)/shard_map/while/body/eval_jaxpr/all_gather | solution.py:151
  15.7 186.0 %all-gather.18.cloned.1.call-start = ((), (), s32[]{:S(2)}) async-start(), calls=%async_computation.13 | async-start | bytes 2359296 | tf_op jit(solution)/shard_map/while/body/eval_jaxpr/all_gather | solution.py:111
  16.3 243.7 %all-gather.20.cloned.1.call-start = ((), (), s32[]{:S(2)}) async-start(), calls=%async_computation.14 | async-start | bytes 2359296 | tf_op jit(solution)/shard_map/while/body/eval_jaxpr/all_gather | solution.py:156
  16.9 352.0 %reduce-scatter.15.cloned.1.call-start = ((), (), s32[]{:S(2)}) async-start(), calls=%async_computation.15 | async-start | bytes 8912896 | tf_op jit(solution)/shard_map/while/body/eval_jaxpr/reduce_scatter | solution.py:217
  275.5 193.5 %reduce-scatter.17.cloned.1.call-start = ((), (), s32[]{:S(2)}) async-start(), calls=%async_computation.16 | async-start | bytes 8912896 | tf_op jit(solution)/shard_map/while/body/eval_jaxpr/reduce_scatter | solution.py:149
  310.6 158.4 %copy-start.51 = (f32[2048]{0:T(1024)S(1)}, f32[2048]{0:T(1024)}, u32[]{:S(2)}) copy-start(f32[2048]{0:T(1024)} %get-tuple-element.1176) | copy-start | bytes 24580 | tf_op jit(solution)/shard_map/while
  310.6 158.4 %copy-start.52 = (f32[2048]{0:T(1024)S(1)}, f32[2048]{0:T(1024)}, u32[]{:S(2)}) copy-start(f32[2048]{0:T(1024)} %get-tuple-element.1177) | copy-start | bytes 24580 | tf_op jit(solution)/shard_map/while
  310.6 158.4 %copy-start.71 = (bf16[2,64,2048]{2,1,0:T(8,128)(2,1)S(1)}, bf16[2,64,2048]{2,1,0:T(8,128)(2,1)}, u32[]{:S(2)}) copy-start(bf16[2,64,2048]{2,1,0:T(8,128)(2,1)} %get-tuple-element.1137) | copy-start | bytes 1572868 | tf_op jit(solution)/shard_map/while
  310.6 160.3 %copy-start.62 = (f32[16]{0:T(128)S(1)}, f32[16]{0:T(128)}, u32[]{:S(2)}) copy-start(f32[16]{0:T(128)} %copy-done.61) | copy-start | bytes 196 | tf_op jit(solution)/shard_map/while
  471.3 59.0 %all-gather.14.cloned.1.call-start = ((), (), s32[]{:S(2)}) async-start(), calls=%async_computation.11 | async-start | bytes 1769472 | tf_op jit(solution)/shard_map/while/body/eval_jaxpr/all_gather | solution.py:110
  472.0 97.2 %all-gather.12.cloned.1.call-start = ((), (), s32[]{:S(2)}) async-start(), calls=%async_computation.10 | async-start | bytes 4456448 | tf_op jit(solution)/shard_map/while/body/eval_jaxpr/all_gather | solution.py:108
  476.8 131.4 %all-gather.16.cloned.1.call-start = ((), (), s32[]{:S(2)}) async-start(), calls=%async_computation.12 | async-start | bytes 4456448 | tf_op jit(solution)/shard_map/while/body/eval_jaxpr/all_gather | solution.py:151
  478.6 186.9 %all-gather.18.cloned.1.call-start = ((), (), s32[]{:S(2)}) async-start(), calls=%async_computation.13 | async-start | bytes 2359296 | tf_op jit(solution)/shard_map/while/body/eval_jaxpr/all_gather | solution.py:111
  479.4 244.5 %all-gather.20.cloned.1.call-start = ((), (), s32[]{:S(2)}) async-start(), calls=%async_computation.14 | async-start | bytes 2359296 | tf_op jit(solution)/shard_map/while/body/eval_jaxpr/all_gather | solution.py:156
  479.9 352.8 %reduce-scatter.15.cloned.1.call-start = ((), (), s32[]{:S(2)}) async-start(), calls=%async_computation.15 | async-start | bytes 8912896 | tf_op jit(solution)/shard_map/while/body/eval_jaxpr/reduce_scatter | solution.py:217
  739.2 193.3 %reduce-scatter.17.cloned.1.call-start = ((), (), s32[]{:S(2)}) async-start(), calls=%async_computation.16 | async-start | bytes 8912896 | tf_op jit(solution)/shard_map/while/body/eval_jaxpr/reduce_scatter | solution.py:149
  776.9 157.6 %copy-start.62 = (f32[16]{0:T(128)S(1)}, f32[16]{0:T(128)}, u32[]{:S(2)}) copy-start(f32[16]{0:T(128)} %copy-done.61) | copy-start | bytes 196 | tf_op jit(solution)/shard_map/while
  936.7 90.9 %reduce-scatter.9.cloned.1.call-start = ((), (), s32[]{:S(2)}) async-start(), calls=%async_computation.7 | async-start | bytes 1179648 | tf_op jit(solution)/shard_map/reduce_scatter | solution.py:262
  937.2 163.2 %reduce-scatter.7.cloned.1.call-start = ((), (), s32[]{:S(2)}) async-start(), calls=%async_computation.6 | async-start | bytes 3538944 | tf_op jit(solution)/shard_map/reduce_scatter | solution.py:260
  937.8 250.4 %reduce-scatter.11.cloned.1.call-start = ((), (), s32[]{:S(2)}) async-start(), calls=%async_computation.8 | async-start | bytes 4718592 | tf_op jit(solution)/shard_map/reduce_scatter | solution.py:261
  938.4 338.0 %reduce-scatter.13.cloned.1.call-start = ((), (), s32[]{:S(2)}) async-start(), calls=%async_computation.9 | async-start | bytes 4718592 | tf_op jit(solution)/shard_map/reduce_scatter | solution.py:263
  1008.2 268.7 %copy-start.65 = (f32[2048]{0:T(1024)}, f32[2048]{0:T(1024)S(1)}, u32[]{:S(2)}) copy-start(f32[2048]{0:T(1024)S(1)} %get-tuple-element.1202) | copy-start | bytes 24580
  (140 other events, 3570.7 us)
Sparse Core Ops, SparseCore 0:
  11.6 54.9 all-gather.13
  68.9 36.5 all-gather.11
  107.2 37.4 all-gather.15
  146.9 54.7 all-gather.17
  203.7 56.2 all-gather.19
  275.6 93.3 reduce-scatter.14
  371.3 97.5 reduce-scatter.16
  474.4 55.7 all-gather.13
  532.6 36.6 all-gather.11
  570.8 37.4 all-gather.15
  610.6 54.8 all-gather.17
  667.5 56.2 all-gather.19
  739.3 93.3 reduce-scatter.14
  835.0 97.5 reduce-scatter.16
Sparse Core Ops, SparseCore 1:
  941.3 75.2 reduce-scatter.8
  1021.4 78.9 reduce-scatter.6
  1104.7 83.4 reduce-scatter.10
  1192.7 83.6 reduce-scatter.12
where the time goes:
time: 1290 us; the launch traced here: 1280 us
  waiting for transfers between devices  912 us (71%)
  blocking collectives  159 us (12%)
  matrix products  136 us (11%)
  other arithmetic  33.8 us (3%)
  local copies, waits for them, and re-layouts  22.1 us (2%)
  between operations  15.8 us (1%)
    reduce_scatter x2, waiting for transfers between devices, micro_step(): lax.psum_scatter(partial_out, 'tensor', scatter_dimension=0, tiled=True)  191 us
    reduce_scatter x2, waiting for transfers between devices, micro_step(): lax.psum_scatter(unit_grad_acts + head_grad_acts, 'tensor', scatter_dimen...  114 us
    all_gather x2, waiting for transfers between devices, micro_step(): lax.all_gather(down_weight, 'dp', axis=1, tiled=True)  103 us
    all_gather x2, waiting for transfers between devices, micro_step(): lax.all_gather(up_weight, 'dp', axis=0, tiled=True)  89.9 us
    reduce_scatter x1, waiting for transfers between devices, shards(): lax.psum_scatter(acc_down, 'dp', scatter_dimension=1, tiled=True)  88.1 us
    reduce_scatter x1, waiting for transfers between devices, shards(): lax.psum_scatter(acc_up, 'dp', scatter_dimension=0, tiled=True)  87.8 us
    all_gather x2, waiting for transfers between devices, micro_step(): lax.all_gather(normed.astype(jnp.bfloat16), 'tensor', axis=0, tiled=True)  77.9 us
    reduce_scatter x1, waiting for transfers between devices, shards(): lax.psum_scatter(acc_attn, 'dp', scatter_dimension=0, tiled=True)  72.9 us
  transfers between devices with their start and end apart: 18, of which 17 were waited for; matrix products, arithmetic and copies ran while one was open for 11% of the time, Pallas kernels for 0%

commit v1 on v0

v1 whole, which is shorter than its diff:
```python
import functools

import jax
import jax.numpy as jnp
import numpy as np
from jax import lax
from jax.experimental import pallas as pl
from jax.experimental.pallas import tpu as pltpu
from jax.sharding import PartitionSpec as P

HEAD_DIM = 64
ROT = 32
EPS = 1e-05
BF = jnp.bfloat16
F32 = jnp.float32

OFFSETS = (0, -1, 1, 2)


def tensor_index(x, zlo, core):
    return (x % 4) * 4 + (zlo % 2) * 2 + core % 2


def dp_index(zhi, y):
    return (zhi % 2) * 4 + y % 4


def tensor_move(dx, dz, dc):
    return [
        (tensor_index(x, z, c), tensor_index(x + dx, z + dz, c + dc))
        for x in range(4)
        for z in range(2)
        for c in range(2)
    ]


def dp_move(dz, dy):
    return [(dp_index(z, y), dp_index(z + dz, y + dy)) for z in range(2) for y in range(4)]


def x_up(a):
    return lax.ppermute(a, "tensor", tensor_move(1, 0, 0))


def x_down(a):
    return lax.ppermute(a, "tensor", tensor_move(-1, 0, 0))


def z_swap(a):
    return lax.ppermute(a, "tensor", tensor_move(0, 1, 0))


def core_swap(a):
    return lax.ppermute(a, "tensor", tensor_move(0, 0, 1))


def y_up(a):
    return lax.ppermute(a, "dp", dp_move(0, 1))


def y_down(a):
    return lax.ppermute(a, "dp", dp_move(0, -1))


def zz_swap(a):
    return lax.ppermute(a, "dp", dp_move(1, 0))


def gather_blocks(a, up, down, swap):
    z = swap(a)
    left_a, right_a = up(a), down(a)
    left_z, right_z = up(z), down(z)
    far_a, far_z = up(left_a), down(right_z)
    return [a, z, left_a, left_z, right_a, right_z, far_a, far_z]


def reduce_blocks(blocks, up, down, swap):
    own_a, own_z, left_a, left_z, right_a, right_z, far_a, far_z = blocks
    from_left, from_right = up(far_a), down(far_z)
    send_up = (right_a.astype(F32) + from_left.astype(F32)).astype(BF)
    send_down = (left_z.astype(F32) + from_right.astype(F32)).astype(BF)
    up_a, up_z = up(send_up), up(right_z)
    down_a, down_z = down(left_a), down(send_down)
    other = own_z.astype(F32) + up_z.astype(F32) + down_z.astype(F32)
    mine = own_a.astype(F32) + up_a.astype(F32) + down_a.astype(F32)
    return mine + swap(other.astype(BF)).astype(F32)


def vmem(count):
    return [pl.BlockSpec(memory_space=pltpu.VMEM)] * count


def smem():
    return pl.BlockSpec(memory_space=pltpu.SMEM)


def params(**kwargs):
    return pltpu.CompilerParams(vmem_limit_bytes=60 * 1024 * 1024, **kwargs)


def cost(flops, nbytes, trans=0):
    return pl.CostEstimate(flops=flops, bytes_accessed=nbytes, transcendentals=trans)


def pre_body(sc, tok, cot, gain, bias, acts_out, cot_out, cotsum, hold):
    total = jnp.zeros(cotsum.shape, F32)
    for s in range(2):
        seq = sc[8] if s == 0 else 1 - sc[8]
        xin = tok[seq].astype(F32)
        centred = xin - jnp.mean(xin, axis=-1, keepdims=True)
        spread = jnp.mean(centred * centred, axis=-1, keepdims=True)
        hold[...] = (centred * lax.rsqrt(spread + EPS) * gain[...] + bias[...]).astype(BF)
        total = total + jnp.sum(cot[seq].astype(F32), axis=0, keepdims=True)
        for r in range(8):
            cols = pl.ds(pl.multiple_of(sc[r] * 256, 256), 256)
            acts_out[s, :, r * 256 : (r + 1) * 256] = hold[:, cols]
            cot_out[s, :, r * 256 : (r + 1) * 256] = cot[seq, :, cols]
    cotsum[...] = total


def pre(sc, tok, cot, gain, bias):
    width = tok.shape[-1]
    return pl.pallas_call(
        pre_body,
        in_specs=[smem()] + vmem(4),
        out_specs=vmem(3),
        out_shape=[
            jax.ShapeDtypeStruct(tok.shape, BF),
            jax.ShapeDtypeStruct(tok.shape, BF),
            jax.ShapeDtypeStruct((1, width), F32),
        ],
        scratch_shapes=[pltpu.VMEM(tok.shape[1:], BF)],
        compiler_params=params(),
        cost_estimate=cost(4000000, 2000000),
        name="pre",
    )(sc, tok, cot, gain, bias)


def post_out_body(sc, tok, branch, extra, out, hold):
    for s in range(2):
        seq = sc[8] if s == 0 else 1 - sc[8]
        for r in range(8):
            cols = pl.ds(pl.multiple_of(sc[r] * 256, 256), 256)
            hold[:, cols] = branch[s, :, r * 256 : (r + 1) * 256].astype(F32)
        out[seq] = (tok[seq].astype(F32) + hold[...] + extra[...]).astype(BF)


def post_out(sc, tok, branch, extra):
    return pl.pallas_call(
        post_out_body,
        in_specs=[smem()] + vmem(3),
        out_specs=pl.BlockSpec(memory_space=pltpu.VMEM),
        out_shape=jax.ShapeDtypeStruct(tok.shape, BF),
        scratch_shapes=[pltpu.VMEM(tok.shape[1:], F32)],
        compiler_params=params(),
        cost_estimate=cost(1000000, 2000000),
        name="post_out",
    )(sc, tok, branch, extra)


def post_grad_body(sc, tok, cot, gnormed, gain, out, sums, hold):
    gain_sum = jnp.zeros((1, gain.shape[1]), F32)
    bias_sum = jnp.zeros((1, gain.shape[1]), F32)
    for s in range(2):
        seq = sc[8] if s == 0 else 1 - sc[8]
        for r in range(8):
            cols = pl.ds(pl.multiple_of(sc[r] * 256, 256), 256)
            hold[:, cols] = gnormed[s, :, r * 256 : (r + 1) * 256].astype(F32)
        gn = hold[...]
        xin = tok[seq].astype(F32)
        centred = xin - jnp.mean(xin, axis=-1, keepdims=True)
        scale = lax.rsqrt(jnp.mean(centred * centred, axis=-1, keepdims=True) + EPS)
        xhat = centred * scale
        e = gn * gain[...]
        mean_e = jnp.mean(e, axis=-1, keepdims=True)
        mean_x = jnp.mean(e * xhat, axis=-1, keepdims=True)
        out[seq] = cot[seq].astype(F32) + (e - mean_e - xhat * mean_x) * scale
        gain_sum = gain_sum + jnp.sum(xhat * gn, axis=0, keepdims=True)
        bias_sum = bias_sum + jnp.sum(gn, axis=0, keepdims=True)
    sums[0:1, :] = gain_sum
    sums[1:2, :] = bias_sum


def post_grad(sc, tok, cot, gnormed, gain):
    width = tok.shape[-1]
    return pl.pallas_call(
        post_grad_body,
        in_specs=[smem()] + vmem(4),
        out_specs=vmem(2),
        out_shape=[jax.ShapeDtypeStruct(tok.shape, F32), jax.ShapeDtypeStruct((2, width), F32)],
        scratch_shapes=[pltpu.VMEM(tok.shape[1:], F32)],
        compiler_params=params(),
        cost_estimate=cost(4000000, 3000000),
        name="post_grad",
    )(sc, tok, cot, gnormed, gain)


def turn(u, cosine, sine_low, sine_high):
    return (
        u * cosine
        + pltpu.roll(u, u.shape[-1] - ROT // 2, 1) * sine_low
        + pltpu.roll(u, ROT // 2, 1) * sine_high
    )


def turn_back(u, cosine, sine_low, sine_high):
    return (
        u * cosine
        - pltpu.roll(u, u.shape[-1] - ROT // 2, 1) * sine_low
        - pltpu.roll(u, ROT // 2, 1) * sine_high
    )


def dot(a, b):
    return lax.dot_general(a, b, (((1,), (0,)), ((), ())), preferred_element_type=F32)


def dot_nt(a, b):
    return lax.dot_general(a, b, (((1,), (1,)), ((), ())), preferred_element_type=F32)


def dot_tn(a, b):
    return lax.dot_general(a, b, (((0,), (0,)), ((), ())), preferred_element_type=F32)


QB = 256


def diagonal(size):
    keys = lax.broadcasted_iota(jnp.int32, (size, size), 0)
    queries = lax.broadcasted_iota(jnp.int32, (size, size), 1)
    return keys <= queries


def attn_fwd_body(sc, qkv, bias, cos_t, low_t, high_t, merged, q_out, k_out, v_out, lse, hold):
    length = qkv.shape[0]
    for r in range(length // 64):
        here = slice(64 * r, 64 * r + 64)
        there = pl.ds(pl.multiple_of(sc[r] * 64, 64), 64)
        tables = (cos_t[here, :], low_t[here, :], high_t[here, :])
        rows = qkv[here, :] + bias[0]
        q_out[0, there, :] = (turn(rows[:, :128], *tables) * (HEAD_DIM**-0.5)).astype(BF)
        k_out[0, there, :] = turn(rows[:, 128:256], *tables).astype(BF)
        v_out[0, there, :] = rows[:, 256:].astype(BF)
    keys = k_out[0]
    values_t = v_out[0].T
    lane = lax.broadcasted_iota(jnp.int32, (QB, 128), 1)
    allowed = diagonal(QB)
    for b in range(length // QB):
        begin, end = b * QB, (b + 1) * QB
        query = q_out[0, begin:end, :]
        for a in range(2):
            only = jnp.where(lane // HEAD_DIM == a, query, jnp.zeros_like(query))
            scores = dot_nt(keys[:end], only)
            low = jnp.where(allowed, scores[begin:], -jnp.inf)
            top = jnp.max(low, axis=0, keepdims=True)
            if b > 0:
                top = jnp.maximum(top, jnp.max(scores[:begin], axis=0, keepdims=True))
            weights = jnp.exp(low - top)
            total = jnp.sum(weights, axis=0, keepdims=True)
            out = dot(values_t[:, begin:end], weights.astype(BF))
            if b > 0:
                weights = jnp.exp(scores[:begin] - top)
                total = total + jnp.sum(weights, axis=0, keepdims=True)
                out = out + dot(values_t[:, :begin], weights.astype(BF))
            out = out * (1.0 / total)
            hold[a * HEAD_DIM : (a + 1) * HEAD_DIM, begin:end] = out[
                a * HEAD_DIM : (a + 1) * HEAD_DIM, :
            ]
            lse[0, a : a + 1, begin:end] = top + jnp.log(total)
    for r in range(length // 128):
        here = slice(128 * r, 128 * r + 128)
        merged_abs = hold[:, here].T.astype(BF)
        for k in range(2):
            to = pl.ds(pl.multiple_of(sc[16 + 2 * r + k] * 64, 64), 64)
            merged[to, :] = merged_abs[64 * k : 64 * k + 64, :]


def attn_fwd(sc, qkv, bias, cos_t, low_t, high_t):
    length = qkv.shape[0]
    whole = lambda shape: pl.BlockSpec(shape, lambda h: (0,) * len(shape))
    saved = pl.BlockSpec((1, length, 128), lambda h: (h, 0, 0))
    saved_shape = jax.ShapeDtypeStruct((2, length, 128), BF)
    return pl.pallas_call(
        attn_fwd_body,
        grid=(2,),
        in_specs=[
            smem(),
            pl.BlockSpec((length, 384), lambda h: (0, h)),
            pl.BlockSpec((1, 1, 384), lambda h: (h, 0, 0)),
            whole((length, 128)),
            whole((length, 128)),
            whole((length, 128)),
        ],
        out_specs=[
            pl.BlockSpec((length, 128), lambda h: (0, h)),
            saved,
            saved,
            saved,
            pl.BlockSpec((1, 2, length), lambda h: (h, 0, 0)),
        ],
        out_shape=[
            jax.ShapeDtypeStruct((length, 256), BF),
            saved_shape,
            saved_shape,
            saved_shape,
            jax.ShapeDtypeStruct((2, 2, length), F32),
        ],
        scratch_shapes=[pltpu.VMEM((128, length), F32)],
        compiler_params=params(),
        cost_estimate=cost(8000000000, 6000000, 4000000),
        name="attn_fwd",
    )(sc, qkv, bias, cos_t, low_t, high_t)


def attn_bwd_body(
    sc, q_in, k_in, v_in, lse, gm_in, cos_t, low_t, high_t, gqkv, colsum, gm_hold, dq_t, dq, dk, dv
):
    length = gm_in.shape[0]
    for r in range(length // 64):
        there = pl.ds(pl.multiple_of(sc[r] * 64, 64), 64)
        gm_hold[there, :] = gm_in[64 * r : 64 * r + 64, :]
    keys = k_in[0]
    values = v_in[0]
    keys_t = keys.T
    dk[...] = jnp.zeros_like(dk)
    dv[...] = jnp.zeros_like(dv)
    lane = lax.broadcasted_iota(jnp.int32, (QB, 128), 1)
    allowed = diagonal(QB)
    for b in range(length // QB):
        begin, end = b * QB, (b + 1) * QB
        query = q_in[0, begin:end, :]
        grad = gm_hold[begin:end, :]
        for a in range(2):
            mine = lane // HEAD_DIM == a
            only = jnp.where(mine, query, jnp.zeros_like(query))
            grad_only = jnp.where(mine, grad, jnp.zeros_like(grad))
            shift = lse[0, a : a + 1, begin:end]
            scores = dot_nt(keys[:end], only)
            dprobs = dot_nt(values[:end], grad_only)
            low_p = jnp.where(allowed, jnp.exp(scores[begin:] - shift), 0.0)
            delta = jnp.sum(low_p * dprobs[begin:], axis=0, keepdims=True)
            if b > 0:
                high_p = jnp.exp(scores[:begin] - shift)
                delta = delta + jnp.sum(high_p * dprobs[:begin], axis=0, keepdims=True)
            low_g = (low_p * (dprobs[begin:] - delta)).astype(BF)
            dv[begin:end, :] += dot(low_p.astype(BF), grad_only)
            dk[begin:end, :] += dot(low_g, only)
            out = dot(keys_t[:, begin:end], low_g)
            if b > 0:
                high_g = (high_p * (dprobs[:begin] - delta)).astype(BF)
                dv[:begin, :] += dot(high_p.astype(BF), grad_only)
                dk[:begin, :] += dot(high_g, only)
                out = out + dot(keys_t[:, :begin], high_g)
            dq_t[a * HEAD_DIM : (a + 1) * HEAD_DIM, begin:end] = out[
                a * HEAD_DIM : (a + 1) * HEAD_DIM, :
            ]
    for r in range(length // 128):
        here = slice(128 * r, 128 * r + 128)
        dq[here, :] = dq_t[:, here].T
    total = jnp.zeros((1, 384), F32)
    for r in range(length // 64):
        here = slice(64 * r, 64 * r + 64)
        there = pl.ds(pl.multiple_of(sc[r] * 64, 64), 64)
        tables = (cos_t[here, :], low_t[here, :], high_t[here, :])
        gq = turn_back(dq[there, :] * (HEAD_DIM**-0.5), *tables)
        gk = turn_back(dk[there, :], *tables)
        rows = jnp.concatenate([gq, gk, dv[there, :]], axis=1).astype(BF)
        gqkv[here, :] = rows
        total = total + jnp.sum(rows.astype(F32), axis=0, keepdims=True)
    colsum[0] = total


def attn_bwd(sc, q, k, v, lse, gm, cos_t, low_t, high_t):
    length = gm.shape[0]
    whole = lambda shape: pl.BlockSpec(shape, lambda h: (0,) * len(shape))
    saved = pl.BlockSpec((1, length, 128), lambda h: (h, 0, 0))
    return pl.pallas_call(
        attn_bwd_body,
        grid=(2,),
        in_specs=[
            smem(),
            saved,
            saved,
            saved,
            pl.BlockSpec((1, 2, length), lambda h: (h, 0, 0)),
            pl.BlockSpec((length, 128), lambda h: (0, h)),
            whole((length, 128)),
            whole((length, 128)),
            whole((length, 128)),
        ],
        out_specs=[
            pl.BlockSpec((length, 384), lambda h: (0, h)),
            pl.BlockSpec((1, 1, 384), lambda h: (h, 0, 0)),
        ],
        out_shape=[
            jax.ShapeDtypeStruct((length, 768), BF),
            jax.ShapeDtypeStruct((2, 1, 384), F32),
        ],
        scratch_shapes=[
            pltpu.VMEM((length, 128), BF),
            pltpu.VMEM((128, length), F32),
            pltpu.VMEM((length, 128), F32),
            pltpu.VMEM((length, 128), F32),
            pltpu.VMEM((length, 128), F32),
        ],
        compiler_params=params(),
        cost_estimate=cost(16000000000, 6000000, 4000000),
        name="attn_bwd",
    )(sc, q, k, v, lse, gm, cos_t, low_t, high_t)


def rotary_tables(positions):
    frequency = 10000.0 ** (-(jnp.arange(ROT // 2, dtype=F32) * 2.0 / ROT))
    angles = positions.astype(F32)[:, None] * frequency[None, :]
    cosine, sine = jnp.cos(angles), jnp.sin(angles)
    one = jnp.ones((positions.shape[0], HEAD_DIM - ROT), F32)
    zero_half, zero = jnp.zeros_like(sine), jnp.zeros_like(one)
    cos_t = jnp.concatenate([cosine, cosine, one] * 2, axis=1)
    low_t = jnp.concatenate([-sine, zero_half, zero] * 2, axis=1)
    high_t = jnp.concatenate([zero_half, sine, zero] * 2, axis=1)
    return cos_t, low_t, high_t


def by_kind(a):
    lead = a.shape[:-1]
    return jnp.swapaxes(a.reshape(lead + (2, 3, HEAD_DIM)), -3, -2).reshape(lead + (384,))


def by_head(a):
    lead = a.shape[:-1]
    return jnp.swapaxes(a.reshape(lead + (3, 2, HEAD_DIM)), -3, -2).reshape(lead + (384,))


def gelu(h):
    return jax.nn.gelu(h, approximate=True)


def after(value, *others):
    return lax.optimization_barrier((value,) + others)[0]


def shards(
    tokens,
    attn_weight,
    attn_bias,
    dense_weight,
    dense_bias,
    up_weight,
    up_bias,
    down_weight,
    down_bias,
    norm_gain,
    norm_bias,
    cotangent,
):
    t, d = lax.axis_index("tensor"), lax.axis_index("dp")
    x, zlo, core = t // 4, (t // 2) % 2, t % 2
    zhi, y = d // 4, d % 4
    features = [((zhi + j) % 2) * 4 + (y + o) % 4 for o in OFFSETS for j in range(2)]
    sc = jnp.stack(features + [core]).astype(jnp.int32)
    row_blocks = [
        4 * ((x + o) % 4) + 2 * ((zlo + j) % 2) + (core + k) % 2
        for o in OFFSETS
        for j in range(2)
        for k in range(2)
    ]
    row_table = jnp.stack(row_blocks).astype(jnp.int32)
    inverse = jnp.zeros((16,), jnp.int32).at[row_table].set(jnp.arange(16, dtype=jnp.int32))
    rows_sc = jnp.concatenate([row_table, inverse])
    positions = (row_table[:, None] * 64 + jnp.arange(64, dtype=jnp.int32)[None, :]).reshape(-1)
    tables = rotary_tables(positions)
    gain_row, bias_row = norm_gain[None, :], norm_bias[None, :]

    first = jnp.concatenate([by_kind(attn_weight), up_weight], axis=1)
    second = jnp.concatenate([dense_weight, down_weight], axis=0)
    biases = jnp.concatenate([by_kind(attn_bias), up_bias])[None, :]
    other_biases = core_swap(biases)

    acts_own, cot_own, cot_sum = pre(sc, tokens, cotangent, gain_row, bias_row)
    acts_piece = jnp.concatenate([acts_own[0], core_swap(acts_own[1])], axis=0)
    cot_piece = jnp.concatenate([cot_own[0], core_swap(cot_own[1])], axis=0)

    first_blocks = gather_blocks(first, y_up, y_down, zz_swap)
    acts_blocks = gather_blocks(acts_piece, x_up, x_down, z_swap)
    second_blocks = gather_blocks(after(second, first_blocks[2], first_blocks[4]), y_up, y_down, zz_swap)
    cot_blocks = gather_blocks(
        after(cot_piece, acts_blocks[2], acts_blocks[4]), x_up, x_down, z_swap
    )
    out_bias_grad = lax.psum(cot_sum[0], ("dp", "tensor"))

    acts = jnp.concatenate(acts_blocks, axis=0)
    w1_own = jnp.concatenate(first_blocks, axis=0)
    w1_other = core_swap(w1_own)
    w_attn = jnp.concatenate([w1_own[:, :384], w1_other[:, :384]], axis=1)
    w_up = jnp.concatenate([w1_own[:, 384:], w1_other[:, 384:]], axis=1)
    b_attn = jnp.concatenate([biases[:, :384], other_biases[:, :384]], axis=0)[:, None, :]
    b_up = jnp.concatenate([biases[:, 384:], other_biases[:, 384:]], axis=1)

    qkv = dot(acts, w_attn)
    merged, q, k, v, lse = attn_fwd(rows_sc, qkv, b_attn, *tables)
    hidden = dot(acts, w_up) + b_up
    active_full, gelu_back = jax.vjp(gelu, hidden)
    active = active_full.astype(BF)

    w2_own = jnp.concatenate(second_blocks, axis=1)
    w2_other = core_swap(w2_own)
    w2 = jnp.concatenate([w2_own, w2_other], axis=0)
    mixed_own = jnp.concatenate([merged[:, :128], active[:, :512]], axis=1)
    mixed_other = jnp.concatenate([merged[:, 128:], active[:, 512:]], axis=1)
    mixed = jnp.concatenate([mixed_own, mixed_other], axis=1)
    partial = dot(mixed, w2).astype(BF)
    branch = reduce_blocks(
        [partial[128 * r : 128 * r + 128] for r in range(8)], x_up, x_down, z_swap
    )
    branch = branch.astype(BF)
    branch_pair = jnp.stack([branch[:64], core_swap(branch[64:])])
    layer_out = post_out(sc, tokens, branch_pair, (dense_bias + down_bias)[None, :])

    gout = jnp.concatenate(cot_blocks, axis=0)
    gmixed = dot_nt(gout, w2)
    gm = jnp.concatenate([gmixed[:, :128], gmixed[:, 640:768]], axis=1).astype(BF)
    gactive = jnp.concatenate([gmixed[:, 128:640], gmixed[:, 768:]], axis=1)
    ghidden = gelu_back(gactive)[0].astype(BF)
    up_sum = jnp.sum(ghidden.astype(F32), axis=0, keepdims=True)

    g2_other = dot_tn(mixed_other, gout).astype(BF)
    g2 = dot_tn(mixed_own, gout) + core_swap(g2_other).astype(F32)
    g2 = g2.astype(BF)
    second_grad = reduce_blocks(
        [g2[:, 256 * r : 256 * r + 256] for r in range(8)], y_up, y_down, zz_swap
    )

    gqkv, attn_sum = attn_bwd(rows_sc, q, k, v, lse, gm, *tables)
    gnormed_part = (dot_nt(gqkv, w_attn) + dot_nt(ghidden, w_up)).astype(BF)
    gnormed = reduce_blocks(
        [gnormed_part[128 * r : 128 * r + 128] for r in range(8)], x_up, x_down, z_swap
    )
    gnormed = gnormed.astype(BF)
    gnormed_pair = jnp.stack([gnormed[:64], core_swap(gnormed[64:])])

    g1_other = dot_tn(acts, jnp.concatenate([gqkv[:, 384:], ghidden[:, 512:]], axis=1)).astype(BF)
    g1 = dot_tn(acts, jnp.concatenate([gqkv[:, :384], ghidden[:, :512]], axis=1))
    g1 = (g1 + core_swap(g1_other).astype(F32)).astype(BF)
    first_grad = reduce_blocks(
        [g1[256 * r : 256 * r + 256] for r in range(8)], y_up, y_down, zz_swap
    )
    sums_own = jnp.concatenate([attn_sum[0], up_sum[:, :512]], axis=1)
    sums_other = jnp.concatenate([attn_sum[1], up_sum[:, 512:]], axis=1)
    bias_grads = lax.psum(sums_own + core_swap(sums_other), "dp")[0]

    grad_tokens, norm_sums = post_grad(sc, tokens, cotangent, gnormed_pair, gain_row)
    norm_sums = lax.psum(norm_sums, ("dp", "tensor"))
    return (
        layer_out,
        grad_tokens,
        by_head(first_grad[:, :384]),
        by_head(bias_grads[:384]),
        second_grad[:128],
        out_bias_grad,
        first_grad[:, 384:],
        bias_grads[384:],
        second_grad[128:],
        out_bias_grad,
        norm_sums[0],
        norm_sums[1],
    )


def solution(mesh):
    in_specs = (
        P("dp", "tensor", None),
        P("dp", "tensor"),
        P("tensor"),
        P("tensor", "dp"),
        P(),
        P("dp", "tensor"),
        P("tensor"),
        P("tensor", "dp"),
        P(),
        P(),
        P(),
        P("dp", "tensor", None),
    )
    out_specs = (
        P("dp", "tensor", None),
        P("dp", "tensor", None),
        P("dp", "tensor"),
        P("tensor"),
        P("tensor", "dp"),
        P(),
        P("dp", "tensor"),
        P("tensor"),
        P("tensor", "dp"),
        P(),
        P(),
        P(),
    )
    return jax.shard_map(shards, mesh=mesh, in_specs=in_specs, out_specs=out_specs, check_vma=False)
```

time: 1290 us -> 484 us (0.38)
  waiting for transfers between devices: 912 us -> 112 us
  starting transfers between devices: 1.14 us -> 75 us
  blocking collectives: 159 us -> 85.4 us
  matrix products: 136 us -> 65.4 us
  local copies, waits for them, and re-layouts: 22.1 us -> 74.5 us
  Pallas kernels: 0 us -> 33.7 us
  between operations: 15.8 us -> 2.1 us
    reduce_scatter x8 -> x0, waiting for transfers between devices: 554 us -> none  [the longest x2 191 us: micro_step(): lax.psum_scatter(partial_out, 'tensor', scatter_dimension=0, tiled=True)]
    all_gather x10 -> x0, waiting for transfers between devices: 352 us -> none  [the longest x2 103 us: micro_step(): lax.all_gather(down_weight, 'dp', axis=1, tiled=True)]
    ppermute x0 -> x66, waiting for transfers between devices: none -> 112 us  [the longest x12 32.8 us: x_down(): return lax.ppermute(a, 'tensor', tensor_move(-1, 0, 0))]
    ppermute x0 -> x66, starting transfers between devices: none -> 75 us  [the longest x12 28.4 us: x_down(): return lax.ppermute(a, 'tensor', tensor_move(-1, 0, 0))]
    all_gather x2 -> x0, blocking collectives: 71 us -> none  [micro_step(): lax.all_gather(dense_weight, 'dp', axis=1, tiled=True)]
    dot_general x48 -> x10, matrix products: 136 us -> 65.4 us  [the longest x3 23.8 us: dot(): lax.dot_general(a, b, (((1,), (0,)), ((), ())), preferred_element_type=F32)]
    pallas_call x0 -> x5, Pallas kernels: none -> 33.7 us  [the longest x1 13.8 us: attn_bwd(): pl.pallas_call(attn_bwd_body, grid=(2,), in_specs=[smem(), saved, saved,...]
    unnamed x13 -> x106, local copies, waits for them, and re-layouts: 0.67 us -> 31.2 us
  transfers between devices with their start and end apart: 18 -> 66, of which waited for: 17 -> 29; matrix products, arithmetic and copies ran while one was open for 11% -> 26% of each run, Pallas kernels for 0% -> 2%
where the time goes in v1:
time: 484 us; the launch traced here: 475 us
  waiting for transfers between devices  112 us (23%)
  blocking collectives  85.4 us (18%)
  starting transfers between devices  75 us (15%)
  local copies, waits for them, and re-layouts  74.5 us (15%)
  matrix products  65.4 us (14%)
  Pallas kernels  33.7 us (7%)
  other arithmetic  26.4 us (5%)
    psum x1, blocking collectives, shards(): out_bias_grad = lax.psum(cot_sum[0], ('dp', 'tensor'))  66.6 us
    ppermute x12, waiting for transfers between devices, x_down(): return lax.ppermute(a, 'tensor', tensor_move(-1, 0, 0))  32.8 us
    unnamed x106, local copies, waits for them, and re-layouts  31.2 us
    ppermute x12, starting transfers between devices, x_down(): return lax.ppermute(a, 'tensor', tensor_move(-1, 0, 0))  28.4 us
    ppermute x12, waiting for transfers between devices, x_up(): return lax.ppermute(a, 'tensor', tensor_move(1, 0, 0))  25.1 us
    ppermute x12, waiting for transfers between devices, y_down(): return lax.ppermute(a, 'dp', dp_move(0, -1))  23.9 us
    dot_general x3, matrix products, dot(): lax.dot_general(a, b, (((1,), (0,)), ((), ())), preferred_element_type=F32)  23.8 us
    ppermute x12, starting transfers between devices, y_up(): return lax.ppermute(a, 'dp', dp_move(0, 1))  23 us
  transfers between devices with their start and end apart: 66, of which 29 were waited for; matrix products, arithmetic and copies ran while one was open for 26% of the time, Pallas kernels for 2%

profile of v1, /device:TPU:24, one launch (start us, length us, event | category | flops | bytes accessed | tf_op | source)
XLA Modules:
  0.0 474.6 jit_solution(14923014803900514400)
XLA Ops:
  60.6 9.9 %collective-permute-done.10 = bf16[256,896]{1,0:T(8,128)(2,1)S(1)} collective-permute-done((bf16[256,896]{1,0:T(8,128)(2,1)}, bf16[256,896]{1,0:T(8,128)(2,1)S(1)}, u32[]{:S(2)}, u32[]{:S(2)}) %collective-permute-start.10) | collective-permute-done | bytes 458784 | tf_op jit(solution)/shard_map/ppermute | solution.py:58
  86.9 4.5 collective-permute-done.3
  102.9 8.9 %collective-permute-done.14 = bf16[256,896]{1,0:T(8,128)(2,1)S(1)} collective-permute-done((bf16[256,896]{1,0:T(8,128)(2,1)S(1)}, bf16[256,896]{1,0:T(8,128)(2,1)S(1)}, u32[]{:S(2)}, u32[]{:S(2)}) %collective-permute-start.14) | collective-permute-done | bytes 458784 | tf_op jit(solution)/shard_map/ppermute | solution.py:62
  127.5 10.7 %collective-permute-done.7 = bf16[128,2048]{1,0:T(8,128)(2,1)S(1)} collective-permute-done((bf16[128,2048]{1,0:T(8,128)(2,1)S(1)}, bf16[128,2048]{1,0:T(8,128)(2,1)S(1)}, u32[]{:S(2)}, u32[]{:S(2)}) %collective-permute-start.7) | collective-permute-done | bytes 524320 | tf_op jit(solution)/shard_map/ppermute | solution.py:46
  139.1 9.0 %collective-permute-done.40 = bf16[128,2048]{1,0:T(8,128)(2,1)S(1)} collective-permute-done((bf16[128,2048]{1,0:T(8,128)(2,1)S(1)}, bf16[128,2048]{1,0:T(8,128)(2,1)S(1)}, u32[]{:S(2)}, u32[]{:S(2)}) %collective-permute-start.40) | collective-permute-done | bytes 524320 | tf_op jit(solution)/shard_map/ppermute | solution.py:46
  148.1 7.1 %fusion.57 = (bf16[1024,1280]{1,0:T(8,128)(2,1)}, f32[1024,1280]{1,0:T(8,128)S(1)}) fusion(bf16[1024,2048]{1,0:T(8,128)(2,1)S(1)} %constant_dynamic-update-slice_fusion.25, bf16[640,2048]{1,0:T(8,128)(2,1)S(1)} %collective-permute-done.24, bf16[640,2048]{1,0:T(8,128)(2,1)S(1)} %constant_dynamic-update-slice_fusion.17), kind=kOutput, calls=%fused_computation.147 | convolution fusion | flops 5380505600 | bytes 17301504 | tf_op jit(solution)/shard_map/dot_general | solution.py:219
  167.1 7.2 %fusion.17.qkv = f32[1024,768]{1,0:T(8,128)} fusion(bf16[1024,2048]{1,0:T(8,128)(2,1)} %constant_dynamic-update-slice_fusion, bf16[2048,384]{1,0:T(8,128)(2,1)S(1)} %slice.296, bf16[2048,384]{1,0:T(8,128)(2,1)S(1)} %copy-done.5), kind=kOutput, calls=%fused_computation.32 | convolution fusion | flops 3227516928 | bytes 10485760 | tf_op jit(solution)/shard_map/dot_general | solution.py:215
  174.3 11.9 %attn_fwd.1 = (bf16[1024,256]{1,0:T(8,128)(2,1)}, bf16[2,1024,128]{2,1,0:T(8,128)(2,1)}, bf16[2,1024,128]{2,1,0:T(8,128)(2,1)}, bf16[2,1024,128]{2,1,0:T(8,128)(2,1)}, f32[2,2,1024]{2,1,0:T(2,128)}) custom-call(s32[32]{0:T(128)} %concatenate.108.sc, f32[1024,768]{1,0:T(8,128)} %fusion.17.qkv, f32[2,1,384]{2,1,0:T(1,128)} %broadcast_in_dim.35.bias, ...), custom_call_target="tpu_custom_call" | custom-call | flops 8000000000 | bytes 6000000 | tf_op jit(solution)/shard_map/attn_fwd/pallas_call | solution.py:284
  187.5 13.8 %attn_bwd.1 = (bf16[1024,768]{1,0:T(8,128)(2,1)}, f32[2,1,384]{2,1,0:T(1,128)}) custom-call(s32[32]{0:T(128)} %concatenate.108.sc, bf16[2,1024,128]{2,1,0:T(8,128)(2,1)} %get-tuple-element.29.q_in, bf16[2,1024,128]{2,1,0:T(8,128)(2,1)} %get-tuple-element.30.k_in, bf16[2,1024,128]{2,1,0:T(8,128)(2,1)} %get-tuple-element.31.v_in, ...), custom_call_target="tpu_custom_call" | custom-call | flops 16000000000 | bytes 6000000 | tf_op jit(solution)/shard_map/attn_bwd/pallas_call | solution.py:378
  208.3 10.7 %convert_reduce_fusion = (f32[1024]{0:T(1024)S(1)}, bf16[1024,1024]{0,1:T(8,128)(2,1)S(1)}, bf16[1024,1024]{0,1:T(8,128)(2,1)S(1)}) fusion(f32[1024]{0:T(1024)S(1)} %bitcast.106, f32[1024,512]{0,1:T(8,128)} %copy.89, f32[1024,512]{0,1:T(8,128)S(1)} %copy-done.4, bf16[1024,2048]{1,0:T(8,128)(2,1)} %constant_dynamic-update-slice_fusion, ...), kind=kOutput, calls=%fused_computation.16 | convolution fusion | flops 4330617856 | bytes 16785408 | tf_op jit(solution)/shard_map/dot_general | solution.py:215
  219.2 7.0 %fusion.8 = f32[1024,2048]{1,0:T(8,128)} fusion(bf16[1024,1024]{0,1:T(8,128)(2,1)S(1)} %get-tuple-element.91, bf16[2048,512]{1,0:T(8,128)(2,1)S(1)} %slice.300, bf16[2048,512]{1,0:T(8,128)(2,1)S(1)} %copy-done.3), kind=kOutput, calls=%fused_computation.23 | convolution fusion | flops 4303355904 | bytes 14680064 | tf_op jit(solution)/shard_map/dot_general | solution.py:219
  226.2 6.0 %add_convert_fusion = bf16[1024,2048]{1,0:T(8,128)(2,1)S(1)} fusion(f32[1024,2048]{1,0:T(8,128)} %fusion.8, bf16[1024,768]{1,0:T(8,128)(2,1)S(1)} %copy-done.9, bf16[2048,384]{1,0:T(8,128)(2,1)S(1)} %copy-done.8, bf16[2048,384]{1,0:T(8,128)(2,1)S(1)} %copy-done.6), kind=kOutput, calls=%fused_computation.1 | convolution fusion | flops 3231711232 | bytes 17301504 | tf_op jit(solution)/shard_map/dot_general | solution.py:219
  236.6 4.3 convolution_convert_fusion.2
  241.0 5.9 %convolution_convert_fusion = bf16[1024,2048]{1,0:T(8,128)(2,1)S(1)} fusion(bf16[640,2048]{1,0:T(8,128)(2,1)S(1)} %copy-done.35, bf16[640,2048]{1,0:T(8,128)(2,1)S(1)} %copy-done.27, bf16[1024,512]{0,1:T(8,128)(2,1)S(1)} %get-tuple-element.150, bf16[1024,128]{0,1:T(8,128)(2,1)S(1)} %copy.75, bf16[1024,512]{0,1:T(8,128)(2,1)S(1)} %get-tuple-element.151, ...), kind=kOutput, calls=%fused_computation.18 | convolution fusion | flops 5391777792 | bytes 12058624 | tf_op jit(solution)/shard_map/dot_general | solution.py:215
  255.8 6.0 %convolution_convert_fusion.1 = bf16[2048,896]{0,1:T(8,128)(2,1)} fusion(bf16[1024,2048]{1,0:T(8,128)(2,1)S(1)} %copy-done.28, bf16[1024,512]{0,1:T(8,128)(2,1)S(1)} %get-tuple-element.122, bf16[1024,384]{0,1:T(8,128)(2,1)S(1)} %copy-done.15), kind=kOutput, calls=%fused_computation.19 | convolution fusion | flops 3763601408 | bytes 9699328 | tf_op jit(solution)/shard_map/dot_general | solution.py:223
  267.6 7.5 %collective-permute-done.41 = bf16[128,2048]{1,0:T(8,128)(2,1)S(1)} collective-permute-done((bf16[128,2048]{1,0:T(8,128)(2,1)S(1)}, bf16[128,2048]{1,0:T(8,128)(2,1)S(1)}, u32[]{:S(2)}, u32[]{:S(2)}) %collective-permute-start.41) | collective-permute-done | bytes 524320 | tf_op jit(solution)/shard_map/ppermute | solution.py:42
  279.7 18.7 %psum.21 = f32[1,896]{1,0:T(1,128)S(1)} all-reduce(f32[1,896]{1,0:T(1,128)S(1)} %maximum_add_fusion), channel_id=1, replica_groups=mesh['dp'=8,'tensor'=16] {'dp'}, use_global_device_ids=true, to_apply=%region_2.3 | all-reduce | flops 896 | bytes 7168 | tf_op jit(solution)/shard_map/psum | solution.py:550
  303.3 4.5 collective-permute-done.46
  317.2 4.0 collective-permute-done.31
  326.2 4.5 collective-permute-done.42
  335.0 4.7 add_convert_fusion.2
  343.2 6.4 %add_convert_fusion.1 = bf16[2048,896]{0,1:T(8,128)(2,1)S(1)} fusion(bf16[2048,896]{0,1:T(8,128)(2,1)} %collective-permute-done.49, bf16[1024,2048]{1,0:T(8,128)(2,1)S(1)} %copy-done.29, bf16[1024,512]{0,1:T(8,128)(2,1)S(1)} %copy-done.11, bf16[1024,384]{0,1:T(8,128)(2,1)S(1)} %copy-done.14), kind=kOutput, calls=%fused_computation.2 | convolution fusion | flops 3767271424 | bytes 13369344 | tf_op jit(solution)/shard_map/dot_general | solution.py:223
  359.5 66.6 %all-reduce = (f32[2048]{0:T(1024)S(1)}, f32[2,2048]{1,0:T(2,128)S(1)}) all-reduce(f32[2048]{0:T(1024)S(1)} %bitcast.103, f32[2,2048]{1,0:T(2,128)} %get-tuple-element.39), channel_id=1, replica_groups=mesh['dp'=8,'tensor'=16] {'dp','tensor'}, use_global_device_ids=true, to_apply=%region_3.4 | all-reduce | flops 6144 | bytes 49152 | tf_op jit(solution)/shard_map/psum | solution.py:490
  442.5 4.4 collective-permute-done.53
  (323 shorter events, 228.1 us)
Async XLA Ops:
  3.9 30.5 %collective-permute-start.9 = (bf16[256,896]{1,0:T(8,128)(2,1)}, bf16[256,896]{1,0:T(8,128)(2,1)}, u32[]{:S(2)}, u32[]{:S(2)}) collective-permute-start(bf16[256,896]{1,0:T(8,128)(2,1)} %get-tuple-element.138), channel_id=1, source_target_pairs={{0,16},{16,32},{32,48},{48,0},{64,80},{80,96},{96,112},{112,64},{1... | collective-permute-start | bytes 1376264 | tf_op jit(solution)/shard_map/ppermute | solution.py:58
  4.1 32.2 %collective-permute-start.8 = (bf16[256,896]{1,0:T(8,128)(2,1)}, bf16[256,896]{1,0:T(8,128)(2,1)}, u32[]{:S(2)}, u32[]{:S(2)}) collective-permute-start(bf16[256,896]{1,0:T(8,128)(2,1)} %get-tuple-element.138), channel_id=1, source_target_pairs={{0,64},{16,80},{32,96},{48,112},{64,0},{80,16},{96,32},{112,48},{1... | collective-permute-start | bytes 1376264 | tf_op jit(solution)/shard_map/ppermute | solution.py:66
  8.0 27.4 %collective-permute-start.11 = (bf16[256,896]{1,0:T(8,128)(2,1)}, bf16[256,896]{1,0:T(8,128)(2,1)}, u32[]{:S(2)}, u32[]{:S(2)}) collective-permute-start(bf16[256,896]{1,0:T(8,128)(2,1)} %get-tuple-element.138), channel_id=1, source_target_pairs={{0,48},{16,0},{32,16},{48,32},{64,112},{80,64},{96,80},{112,96},{1... | collective-permute-start | bytes 1376264 | tf_op jit(solution)/shard_map/ppermute | solution.py:62
  35.5 46.8 %collective-permute-start.20 = (bf16[640,256]{1,0:T(8,128)(2,1)S(1)}, bf16[640,256]{1,0:T(8,128)(2,1)S(1)}, u32[]{:S(2)}, u32[]{:S(2)}) collective-permute-start(bf16[640,256]{1,0:T(8,128)(2,1)S(1)} %pad_maximum_fusion.16), channel_id=1, source_target_pairs={{0,48},{16,0},{32,16},{48,32},{64,112},{80,64},{96,80},{112,96},{1... | collective-permute-start | bytes 983048 | tf_op jit(solution)/shard_map/ppermute | solution.py:62
  48.8 28.0 %collective-permute-start.13 = (bf16[256,896]{1,0:T(8,128)(2,1)}, bf16[256,896]{1,0:T(8,128)(2,1)S(1)}, u32[]{:S(2)}, u32[]{:S(2)}) collective-permute-start(bf16[256,896]{1,0:T(8,128)(2,1)} %collective-permute-done.9), channel_id=1, source_target_pairs={{0,16},{16,32},{32,48},{48,0},{64,80},{80,96},{96,112},{112,64},{1... | collective-permute-start | bytes 1376264 | tf_op jit(solution)/shard_map/ppermute | solution.py:58
  56.8 67.3 %collective-permute-start.37 = (bf16[128,2048]{1,0:T(8,128)(2,1)S(1)}, bf16[128,2048]{1,0:T(8,128)(2,1)S(1)}, u32[]{:S(2)}, u32[]{:S(2)}) collective-permute-start(bf16[128,2048]{1,0:T(8,128)(2,1)S(1)} %pad_maximum_fusion.12), channel_id=1, source_target_pairs={{0,12},{1,13},{2,14},{3,15},{4,0},{5,1},{6,2},{7,3},{8,4},{9,5},{1... | collective-permute-start | bytes 1572872 | tf_op jit(solution)/shard_map/ppermute | solution.py:46
  95.7 52.5 %collective-permute-start.24 = (bf16[640,2048]{1,0:T(8,128)(2,1)S(1)}, bf16[640,2048]{1,0:T(8,128)(2,1)S(1)}, u32[]{:S(2)}, u32[]{:S(2)}) collective-permute-start(bf16[640,2048]{1,0:T(8,128)(2,1)S(1)} %constant_dynamic-update-slice_fusion.17), channel_id=1, source_target_pairs={{0,1},{1,0},{2,3},{3,2},{4,5},{5,4},{6,7},{7,6},{8,9},{9,8},{10,11... | collective-permute-start | bytes 7864328 | tf_op jit(solution)/shard_map/ppermute | solution.py:54
  116.6 47.7 %collective-permute-start.15 = (bf16[2048,896]{1,0:T(8,128)(2,1)}, bf16[2048,896]{1,0:T(8,128)(2,1)}, u32[]{:S(2)}, u32[]{:S(2)}) collective-permute-start(bf16[2048,896]{1,0:T(8,128)(2,1)} %constant_dynamic-update-slice_fusion.9), channel_id=1, source_target_pairs={{0,1},{1,0},{2,3},{3,2},{4,5},{5,4},{6,7},{7,6},{8,9},{9,8},{10,11... | collective-permute-start | bytes 11010056 | tf_op jit(solution)/shard_map/ppermute | solution.py:54
  219.1 60.6 %collective-permute-start.57 = (f32[1,896]{1,0:T(1,128)S(1)}, f32[1,896]{1,0:T(1,128)S(1)}, u32[]{:S(2)}, u32[]{:S(2)}) collective-permute-start(f32[1,896]{1,0:T(1,128)S(1)} %pad_maximum_fusion.19), channel_id=1, source_target_pairs={{0,1},{1,0},{2,3},{3,2},{4,5},{5,4},{6,7},{7,6},{8,9},{9,8},{10,11... | collective-permute-start | bytes 10760 | tf_op jit(solution)/shard_map/ppermute | solution.py:54
  252.4 22.8 %collective-permute-start.41 = (bf16[128,2048]{1,0:T(8,128)(2,1)S(1)}, bf16[128,2048]{1,0:T(8,128)(2,1)S(1)}, u32[]{:S(2)}, u32[]{:S(2)}) collective-permute-start(bf16[128,2048]{1,0:T(8,128)(2,1)S(1)} %get-tuple-element.97), channel_id=1, source_target_pairs={{0,4},{1,5},{2,6},{3,7},{4,8},{5,9},{6,10},{7,11},{8,12},{9,13},{1... | collective-permute-start | bytes 1572872 | tf_op jit(solution)/shard_map/ppermute | solution.py:42
  252.4 22.8 %collective-permute-start.45 = (bf16[128,2048]{1,0:T(8,128)(2,1)S(1)}, bf16[128,2048]{1,0:T(8,128)(2,1)S(1)}, u32[]{:S(2)}, u32[]{:S(2)}) collective-permute-start(bf16[128,2048]{1,0:T(8,128)(2,1)S(1)} %get-tuple-element.98), channel_id=1, source_target_pairs={{0,12},{1,13},{2,14},{3,15},{4,0},{5,1},{6,2},{7,3},{8,4},{9,5},{1... | collective-permute-start | bytes 1572872 | tf_op jit(solution)/shard_map/ppermute | solution.py:46
  263.9 34.5 %collective-permute-start.28 = (bf16[128,2048]{1,0:T(8,128)(2,1)}, bf16[128,2048]{1,0:T(8,128)(2,1)S(1)}, u32[]{:S(2)}, u32[]{:S(2)}) collective-permute-start(bf16[128,2048]{1,0:T(8,128)(2,1)} %get-tuple-element.105), channel_id=1, source_target_pairs={{0,4},{1,5},{2,6},{3,7},{4,8},{5,9},{6,10},{7,11},{8,12},{9,13},{1... | collective-permute-start | bytes 1572872 | tf_op jit(solution)/shard_map/ppermute | solution.py:42
  263.9 47.7 %collective-permute-start.27 = (bf16[128,2048]{1,0:T(8,128)(2,1)}, bf16[128,2048]{1,0:T(8,128)(2,1)S(1)}, u32[]{:S(2)}, u32[]{:S(2)}) collective-permute-start(bf16[128,2048]{1,0:T(8,128)(2,1)} %get-tuple-element.106), channel_id=1, source_target_pairs={{0,12},{1,13},{2,14},{3,15},{4,0},{5,1},{6,2},{7,3},{8,4},{9,5},{1... | collective-permute-start | bytes 1572872 | tf_op jit(solution)/shard_map/ppermute | solution.py:46
  275.2 26.1 %collective-permute-start.44 = (bf16[128,2048]{1,0:T(8,128)(2,1)}, bf16[128,2048]{1,0:T(8,128)(2,1)S(1)}, u32[]{:S(2)}, u32[]{:S(2)}) collective-permute-start(bf16[128,2048]{1,0:T(8,128)(2,1)} %get-tuple-element.99), channel_id=1, source_target_pairs={{0,4},{1,5},{2,6},{3,7},{4,8},{5,9},{6,10},{7,11},{8,12},{9,13},{1... | collective-permute-start | bytes 1572872 | tf_op jit(solution)/shard_map/ppermute | solution.py:42
  275.2 23.3 %collective-permute-start.30 = (bf16[128,2048]{1,0:T(8,128)(2,1)S(1)}, bf16[128,2048]{1,0:T(8,128)(2,1)}, u32[]{:S(2)}, u32[]{:S(2)}) collective-permute-start(bf16[128,2048]{1,0:T(8,128)(2,1)S(1)} %get-tuple-element.102), channel_id=1, source_target_pairs={{0,12},{1,13},{2,14},{3,15},{4,0},{5,1},{6,2},{7,3},{8,4},{9,5},{1... | collective-permute-start | bytes 1572872 | tf_op jit(solution)/shard_map/ppermute | solution.py:46
  279.7 28.1 %collective-permute-start.46 = (bf16[128,2048]{1,0:T(8,128)(2,1)}, bf16[128,2048]{1,0:T(8,128)(2,1)}, u32[]{:S(2)}, u32[]{:S(2)}) collective-permute-start(bf16[128,2048]{1,0:T(8,128)(2,1)} %get-tuple-element.96), channel_id=1, source_target_pairs={{0,12},{1,13},{2,14},{3,15},{4,0},{5,1},{6,2},{7,3},{8,4},{9,5},{1... | collective-permute-start | bytes 1572872 | tf_op jit(solution)/shard_map/ppermute | solution.py:46
  298.4 36.6 %collective-permute-start.58 = (bf16[640,2048]{1,0:T(8,128)(2,1)}, bf16[640,2048]{1,0:T(8,128)(2,1)}, u32[]{:S(2)}, u32[]{:S(2)}) collective-permute-start(bf16[640,2048]{1,0:T(8,128)(2,1)} %convolution_convert_fusion.2), channel_id=1, source_target_pairs={{0,1},{1,0},{2,3},{3,2},{4,5},{5,4},{6,7},{7,6},{8,9},{9,8},{10,11... | collective-permute-start | bytes 7864328 | tf_op jit(solution)/shard_map/ppermute | solution.py:54
  298.5 44.6 %collective-permute-start.49 = (bf16[2048,896]{0,1:T(8,128)(2,1)}, bf16[2048,896]{0,1:T(8,128)(2,1)}, u32[]{:S(2)}, u32[]{:S(2)}) collective-permute-start(bf16[2048,896]{0,1:T(8,128)(2,1)} %convolution_convert_fusion.1), channel_id=1, source_target_pairs={{0,1},{1,0},{2,3},{3,2},{4,5},{5,4},{6,7},{7,6},{8,9},{9,8},{10,11... | collective-permute-start | bytes 11010056 | tf_op jit(solution)/shard_map/ppermute | solution.py:54
  326.2 126.5 %collective-permute-start.32 = (bf16[64,2048]{1,0:T(8,128)(2,1)}, bf16[64,2048]{1,0:T(8,128)(2,1)}, u32[]{:S(2)}, u32[]{:S(2)}) collective-permute-start(bf16[64,2048]{1,0:T(8,128)(2,1)} %get-tuple-element.132), channel_id=1, source_target_pairs={{0,1},{1,0},{2,3},{3,2},{4,5},{5,4},{6,7},{7,6},{8,9},{9,8},{10,11... | collective-permute-start | bytes 786440 | tf_op jit(solution)/shard_map/ppermute | solution.py:54
  340.9 85.3 %collective-permute-start.59 = (bf16[640,256]{1,0:T(8,128)(2,1)}, bf16[640,256]{1,0:T(8,128)(2,1)}, u32[]{:S(2)}, u32[]{:S(2)}) collective-permute-start(bf16[640,256]{1,0:T(8,128)(2,1)} %get-tuple-element.115), channel_id=1, source_target_pairs={{0,16},{16,32},{32,48},{48,0},{64,80},{80,96},{96,112},{112,64},{1... | collective-permute-start | bytes 983048 | tf_op jit(solution)/shard_map/ppermute | solution.py:58
  342.5 85.3 %collective-permute-start.63 = (bf16[640,256]{1,0:T(8,128)(2,1)}, bf16[640,256]{1,0:T(8,128)(2,1)}, u32[]{:S(2)}, u32[]{:S(2)}) collective-permute-start(bf16[640,256]{1,0:T(8,128)(2,1)} %get-tuple-element.116), channel_id=1, source_target_pairs={{0,48},{16,0},{32,16},{48,32},{64,112},{80,64},{96,80},{112,96},{1... | collective-permute-start | bytes 983048 | tf_op jit(solution)/shard_map/ppermute | solution.py:62
  352.6 77.6 %collective-permute-start.50 = (bf16[256,896]{0,1:T(8,128)(2,1)}, bf16[256,896]{0,1:T(8,128)(2,1)}, u32[]{:S(2)}, u32[]{:S(2)}) collective-permute-start(bf16[256,896]{0,1:T(8,128)(2,1)} %get-tuple-element.109), channel_id=1, source_target_pairs={{0,16},{16,32},{32,48},{48,0},{64,80},{80,96},{96,112},{112,64},{1... | collective-permute-start | bytes 1376264 | tf_op jit(solution)/shard_map/ppermute | solution.py:58
  355.4 77.6 %collective-permute-start.54 = (bf16[256,896]{0,1:T(8,128)(2,1)}, bf16[256,896]{0,1:T(8,128)(2,1)}, u32[]{:S(2)}, u32[]{:S(2)}) collective-permute-start(bf16[256,896]{0,1:T(8,128)(2,1)} %get-tuple-element.110), channel_id=1, source_target_pairs={{0,48},{16,0},{32,16},{48,32},{64,112},{80,64},{96,80},{112,96},{1... | collective-permute-start | bytes 1376264 | tf_op jit(solution)/shard_map/ppermute | solution.py:62
  441.6 22.8 %collective-permute-start.60 = (bf16[640,256]{1,0:T(8,128)(2,1)}, bf16[640,256]{1,0:T(8,128)(2,1)}, u32[]{:S(2)}, u32[]{:S(2)}) collective-permute-start(bf16[640,256]{1,0:T(8,128)(2,1)} %get-tuple-element.113), channel_id=1, source_target_pairs={{0,16},{16,32},{32,48},{48,0},{64,80},{80,96},{96,112},{112,64},{1... | collective-permute-start | bytes 983048 | tf_op jit(solution)/shard_map/ppermute | solution.py:58
  (78 other events, 1107.0 us)
